TPU v7x, 32 devices: a whole 2x2x4 slice. The times are simulated.
32 devices in a mesh: dp: 8 (over y, x, core), seq: 4 (over z).
Axes of the slice: x: 2, y: 2, z: 4, core: 2. Of those that a mesh axis runs over, the one named last changes fastest.
Arguments:
- inputs: bfloat16 [3, 8, 1024, 1024], P(None, 'dp', 'seq'), may hold values from -6 to 6
- upstream: bfloat16 [3, 8, 1024, 1024], P(None, 'dp', 'seq'), may hold values from -6 to 6
- norm_gain: float32 [1024], replicated, may hold values from 0.5 to 1.5
- query_weight: bfloat16 [1024, 1024], P('dp', 'seq'), may hold values from -0.1875 to 0.1875
- key_weight: bfloat16 [1024, 1024], P('dp', 'seq'), may hold values from -0.1875 to 0.1875
- value_weight: bfloat16 [1024, 2048], P('dp', 'seq'), may hold values from -0.1875 to 0.1875
- gate_weight: bfloat16 [1024, 2048], P('dp', 'seq'), may hold values from -0.1875 to 0.1875
- rate_weight: bfloat16 [1024, 16], P('dp', 'seq'), may hold values from -0.1875 to 0.1875
- conv_weight: float32 [4, 4096], replicated, may hold values from -2.5 to 2.5
- decay_log: float32 [8], replicated, may hold values from -7 to -2
- decay_bias: float32 [8], replicated, may hold values from -1 to 1
- out_gain: float32 [256], replicated, may hold values from 0.5 to 1.5
- output_weight: bfloat16 [2048, 1024], P('dp', 'seq'), may hold values from -0.125 to 0.125
- ffn_gain: float32 [1024], replicated, may hold values from 0.5 to 1.5
- ffn_gate: bfloat16 [1024, 2816], P('dp', 'seq'), may hold values from -0.1875 to 0.1875
- ffn_up: bfloat16 [1024, 2816], P('dp', 'seq'), may hold values from -0.1875 to 0.1875
- ffn_down: bfloat16 [2816, 1024], P('dp', 'seq'), may hold values from -0.109375 to 0.109375
Outputs:
- outputs: bfloat16 [3, 8, 1024, 1024], P(None, 'dp', 'seq')
- input_grad: float32 [3, 8, 1024, 1024], P(None, 'dp', 'seq')
- norm_gain_grad: float32 [1024], replicated
- query_weight_grad: float32 [1024, 1024], P('dp', 'seq')
- key_weight_grad: float32 [1024, 1024], P('dp', 'seq')
- value_weight_grad: float32 [1024, 2048], P('dp', 'seq')
- gate_weight_grad: float32 [1024, 2048], P('dp', 'seq')
- rate_weight_grad: float32 [1024, 16], P('dp', 'seq')
- conv_weight_grad: float32 [4, 4096], replicated
- decay_log_grad: float32 [8], replicated
- decay_bias_grad: float32 [8], replicated
- out_gain_grad: float32 [256], replicated
- output_weight_grad: float32 [2048, 1024], P('dp', 'seq')
- ffn_gain_grad: float32 [1024], replicated
- ffn_gate_grad: float32 [1024, 2816], P('dp', 'seq')
- ffn_up_grad: float32 [1024, 2816], P('dp', 'seq')
- ffn_down_grad: float32 [2816, 1024], P('dp', 'seq')
All inputs are finite; a program needn't handle non-finite values.
Results may differ from a plain program's by a relative error of at most 0.017.
Values may be sent and summed in bfloat16 or wider, within the bound.
A program may use at most 512 MiB of HBM per device.

v0:
```python
import jax
import jax.numpy as jnp
from jax import lax
from jax.sharding import PartitionSpec as P

GROUP = 64


EPSILON = 1e-06


def passed_along(block, axis, distance):
    devices = range(lax.axis_size(axis))
    route = [(i - distance, i) for i in devices if i - distance in devices]
    return lax.ppermute(block, axis, route)


def high_dot(left_mat, right_mat):
    return jnp.dot(
        left_mat, right_mat, precision=lax.Precision.HIGHEST, preferred_element_type=jnp.float32
    )


def plain_dot(left_mat, right_mat):
    return jnp.dot(left_mat, right_mat, preferred_element_type=jnp.float32)


def back_dot(left_mat, right_mat):
    return lax.dot_general(
        left_mat, right_mat, (((1,), (1,)), ((), ())), preferred_element_type=jnp.float32
    )


def weight_dot(left_mat, right_mat):
    return lax.dot_general(
        left_mat, right_mat, (((0,), (0,)), ((), ())), preferred_element_type=jnp.float32
    )


def batch_apply(left_mat, right_mat, formula):
    return jnp.einsum(formula, left_mat, right_mat, precision=lax.Precision.HIGHEST)


def rms_scale(values, gain_vec):
    return (
        values * lax.rsqrt(jnp.mean(values * values, axis=-1, keepdims=True) + EPSILON) * gain_vec
    )


def swiglu_product(gate_vals, up_vals):
    return jax.nn.silu(gate_vals) * up_vals


def gate_output(mixture, gate_pre, out_gain):
    head_count = mixture.shape[-2]
    gated_rows = rms_scale(mixture, out_gain) * jax.nn.silu(
        gate_pre.reshape(gate_pre.shape[:-1] + (head_count, -1))
    )
    return gated_rows.reshape(gate_pre.shape)


def prepare(query_ext, key_ext, value_ext, rate_pre, conv_weight, decay_log, decay_bias):
    conv_lead = conv_weight.shape[0] - 1
    length = query_ext.shape[1] - conv_lead
    head_count = decay_log.shape[0]
    query_width = query_ext.shape[2]
    key_dim = query_width // head_count
    batch_size = query_ext.shape[0]

    def convolve(extended, kernel):
        summed_taps = kernel[0] * extended[:, 0:length]
        for offset_idx in range(1, conv_lead + 1):
            summed_taps = (
                summed_taps + kernel[offset_idx] * extended[:, offset_idx : offset_idx + length]
            )
        return jax.nn.silu(summed_taps)

    queries = convolve(query_ext, conv_weight[:, :query_width]).reshape(
        batch_size, length, head_count, key_dim
    )
    key_rows = convolve(key_ext, conv_weight[:, query_width : 2 * query_width]).reshape(
        batch_size, length, head_count, key_dim
    )
    values = convolve(value_ext, conv_weight[:, 2 * query_width :]).reshape(
        batch_size, length, head_count, -1
    )
    queries = (
        queries
        * lax.rsqrt(jnp.sum(queries * queries, axis=-1, keepdims=True) + EPSILON)
        * key_dim ** (-0.5)
    )
    key_rows = key_rows * lax.rsqrt(jnp.sum(key_rows * key_rows, axis=-1, keepdims=True) + EPSILON)
    beta_rows = jax.nn.sigmoid(rate_pre[..., head_count:])
    decays = -jnp.exp(decay_log) * jax.nn.softplus(rate_pre[..., :head_count] + decay_bias)
    return (queries, key_rows, values, beta_rows, decays)


def group_terms(queries, key_rows, values, beta_rows, decays):
    group_len = decays.shape[0]
    cumulative = jnp.cumsum(decays)
    row_index = lax.broadcasted_iota(jnp.int32, (group_len, group_len), 0)
    col_index = lax.broadcasted_iota(jnp.int32, (group_len, group_len), 1)
    strict_lower = row_index > col_index
    lower_incl = row_index >= col_index
    decay_ratio = jnp.exp(jnp.where(lower_incl, cumulative[:, None] - cumulative[None, :], 0.0))
    mixing = jnp.where(
        strict_lower, beta_rows[:, None] * high_dot(key_rows, key_rows.T) * decay_ratio, 0.0
    )
    identity = jnp.eye(group_len, dtype=jnp.float32)
    inverse = identity - mixing
    powered = mixing
    covered = 2
    while covered < group_len:
        powered = high_dot(powered, powered)
        inverse = high_dot(inverse, identity + powered)
        covered = covered * 2
    solved = inverse * beta_rows[None, :]
    growth = jnp.exp(cumulative)
    wy_keys = high_dot(solved, growth[:, None] * key_rows)
    wy_values = high_dot(solved, values)
    scores = jnp.where(lower_incl, high_dot(queries, key_rows.T) * decay_ratio, 0.0)
    tail_keys = jnp.exp(cumulative[-1] - cumulative)[:, None] * key_rows
    return (growth, wy_keys, wy_values, scores, tail_keys)


def segment_terms(queries, key_rows, values, beta_rows, decays):
    group_count = queries.shape[0] // GROUP
    key_dim = queries.shape[1]
    value_dim = values.shape[1]
    group_data = (
        queries.reshape(group_count, GROUP, key_dim),
        key_rows.reshape(group_count, GROUP, key_dim),
        values.reshape(group_count, GROUP, value_dim),
        beta_rows.reshape(group_count, GROUP),
        decays.reshape(group_count, GROUP),
    )

    def group_step(carried_maps, group_block):
        mapping, offset = carried_maps
        group_query, group_keys, group_values, group_betas, group_decays = group_block
        growth, wy_keys, wy_values, scores, tail_keys = group_terms(
            group_query, group_keys, group_values, group_betas, group_decays
        )
        fresh_values = wy_values - high_dot(wy_keys, offset)
        result = growth[:, None] * high_dot(group_query, offset) + high_dot(scores, fresh_values)
        carried = high_dot(growth[:, None] * group_query - high_dot(scores, wy_keys), mapping)
        offset = growth[-1] * offset + high_dot(tail_keys.T, fresh_values)
        mapping = growth[-1] * mapping - high_dot(tail_keys.T, high_dot(wy_keys, mapping))
        return ((mapping, offset), (result, carried))

    initial = (jnp.eye(key_dim, dtype=jnp.float32), jnp.zeros((key_dim, value_dim), jnp.float32))
    (mapping, offset), (results, carried) = lax.scan(group_step, initial, group_data)
    return (results.reshape(-1, value_dim), carried.reshape(-1, key_dim), mapping, offset)


def round_trip(values):
    return values.astype(jnp.bfloat16).astype(jnp.float32)


def gather_block(
    query_weight,
    key_weight,
    value_weight,
    gate_weight,
    rate_weight,
    output_weight,
    ffn_gate,
    ffn_up,
    ffn_down,
):
    columns = (
        lax.all_gather(query_weight, "seq", axis=1, tiled=True),
        lax.all_gather(key_weight, "seq", axis=1, tiled=True),
        lax.all_gather(value_weight, "seq", axis=1, tiled=True),
        lax.all_gather(gate_weight, "seq", axis=1, tiled=True),
        lax.all_gather(rate_weight, "seq", axis=1, tiled=True),
        lax.all_gather(output_weight, "seq", axis=1, tiled=True),
        lax.all_gather(ffn_gate, "seq", axis=1, tiled=True),
        lax.all_gather(ffn_up, "seq", axis=1, tiled=True),
        lax.all_gather(ffn_down, "seq", axis=1, tiled=True),
    )
    return (
        lax.all_gather(columns[0], "dp", axis=0, tiled=True),
        lax.all_gather(columns[1], "dp", axis=0, tiled=True),
        lax.all_gather(columns[2], "dp", axis=0, tiled=True),
        lax.all_gather(columns[3], "dp", axis=0, tiled=True),
        lax.all_gather(columns[4], "dp", axis=0, tiled=True),
        lax.all_gather(columns[5], "dp", axis=0, tiled=True),
        lax.all_gather(columns[6], "dp", axis=0, tiled=True),
        lax.all_gather(columns[7], "dp", axis=0, tiled=True),
        lax.all_gather(columns[8], "dp", axis=0, tiled=True),
    )


def sum_block(
    grad_query,
    grad_key,
    grad_value,
    grad_gate,
    grad_rate,
    grad_output,
    grad_ffgate,
    grad_ffup,
    grad_down,
):
    summed_rows = (
        lax.psum_scatter(grad_query, "dp", scatter_dimension=0, tiled=True),
        lax.psum_scatter(grad_key, "dp", scatter_dimension=0, tiled=True),
        lax.psum_scatter(grad_value, "dp", scatter_dimension=0, tiled=True),
        lax.psum_scatter(grad_gate, "dp", scatter_dimension=0, tiled=True),
        lax.psum_scatter(grad_rate, "dp", scatter_dimension=0, tiled=True),
        lax.psum_scatter(grad_output, "dp", scatter_dimension=0, tiled=True),
        lax.psum_scatter(grad_ffgate, "dp", scatter_dimension=0, tiled=True),
        lax.psum_scatter(grad_ffup, "dp", scatter_dimension=0, tiled=True),
        lax.psum_scatter(grad_down, "dp", scatter_dimension=0, tiled=True),
    )
    return (
        lax.psum_scatter(summed_rows[0], "seq", scatter_dimension=1, tiled=True),
        lax.psum_scatter(summed_rows[1], "seq", scatter_dimension=1, tiled=True),
        lax.psum_scatter(summed_rows[2], "seq", scatter_dimension=1, tiled=True),
        lax.psum_scatter(summed_rows[3], "seq", scatter_dimension=1, tiled=True),
        lax.psum_scatter(summed_rows[4], "seq", scatter_dimension=1, tiled=True),
        lax.psum_scatter(summed_rows[5], "seq", scatter_dimension=1, tiled=True),
        lax.psum_scatter(summed_rows[6], "seq", scatter_dimension=1, tiled=True),
        lax.psum_scatter(summed_rows[7], "seq", scatter_dimension=1, tiled=True),
        lax.psum_scatter(summed_rows[8], "seq", scatter_dimension=1, tiled=True),
    )


def shards(
    inputs,
    upstream,
    norm_gain,
    query_weight,
    key_weight,
    value_weight,
    gate_weight,
    rate_weight,
    conv_weight,
    decay_log,
    decay_bias,
    out_gain,
    output_weight,
    ffn_gain,
    ffn_gate,
    ffn_up,
    ffn_down,
):
    batch_count = inputs.shape[0] * inputs.shape[1]
    segment_len = inputs.shape[2]
    model_width = inputs.shape[3]
    row_count = batch_count * segment_len
    conv_lead = conv_weight.shape[0] - 1
    key_width = query_weight.shape[1] * lax.axis_size("seq")
    value_width = value_weight.shape[1] * lax.axis_size("seq")
    tokens = inputs.reshape(row_count, model_width).astype(jnp.float32)
    gathered = gather_block(
        query_weight,
        key_weight,
        value_weight,
        gate_weight,
        rate_weight,
        output_weight,
        ffn_gate,
        ffn_up,
        ffn_down,
    )
    w_query, w_key, w_value, w_gate, w_rate, w_output, w_ffgate, w_ffup, w_ffdown = gathered
    normed_full, norm_back = jax.vjp(rms_scale, tokens, norm_gain)
    normed = normed_full.astype(jnp.bfloat16)
    query_pre = (
        plain_dot(normed, w_query).astype(jnp.bfloat16).reshape(batch_count, segment_len, key_width)
    )
    key_pre = (
        plain_dot(normed, w_key).astype(jnp.bfloat16).reshape(batch_count, segment_len, key_width)
    )
    value_pre = (
        plain_dot(normed, w_value)
        .astype(jnp.bfloat16)
        .reshape(batch_count, segment_len, value_width)
    )
    gate_pre = plain_dot(normed, w_gate)
    rate_pre = plain_dot(normed, w_rate)
    behind = passed_along(
        (
            query_pre[:, segment_len - conv_lead :],
            key_pre[:, segment_len - conv_lead :],
            value_pre[:, segment_len - conv_lead :],
        ),
        "seq",
        1,
    )
    query_ext = jnp.concatenate([behind[0], query_pre], axis=1).astype(jnp.float32)
    key_ext = jnp.concatenate([behind[1], key_pre], axis=1).astype(jnp.float32)
    value_ext = jnp.concatenate([behind[2], value_pre], axis=1).astype(jnp.float32)
    prepared, prep_back = jax.vjp(
        prepare,
        query_ext,
        key_ext,
        value_ext,
        rate_pre.reshape(batch_count, segment_len, -1),
        conv_weight,
        decay_log,
        decay_bias,
    )
    queries, key_rows, values, beta_rows, decays = prepared
    queries = round_trip(queries)
    key_rows = round_trip(key_rows)
    values = round_trip(values)
    segment_map = jax.vmap(jax.vmap(segment_terms))
    (local_out, carried, mapping, offset), seg_back = jax.vjp(
        segment_map,
        queries.transpose(0, 2, 1, 3),
        key_rows.transpose(0, 2, 1, 3),
        values.transpose(0, 2, 1, 3),
        beta_rows.transpose(0, 2, 1),
        decays.transpose(0, 2, 1),
    )
    entering = jnp.zeros_like(offset)
    for hop_index in range(lax.axis_size("seq") - 1):
        entering = passed_along(
            batch_apply(mapping, entering, "shij,shjk->shik") + offset, "seq", 1
        )
    mixture = local_out + batch_apply(carried, entering, "shtk,shkv->shtv")
    gated_full, gate_back = jax.vjp(
        gate_output,
        mixture.transpose(0, 2, 1, 3),
        gate_pre.reshape(batch_count, segment_len, value_width),
        out_gain,
    )
    gated = gated_full.reshape(row_count, value_width).astype(jnp.bfloat16)
    hidden = tokens + plain_dot(gated, w_output)
    normed_two_full, norm_two_back = jax.vjp(rms_scale, hidden, ffn_gain)
    normed_two = normed_two_full.astype(jnp.bfloat16)
    gate_vals = plain_dot(normed_two, w_ffgate)
    up_vals = plain_dot(normed_two, w_ffup)
    product_full, swiglu_back = jax.vjp(swiglu_product, gate_vals, up_vals)
    product = product_full.astype(jnp.bfloat16)
    outputs = (hidden + plain_dot(product, w_ffdown)).astype(jnp.bfloat16).reshape(inputs.shape)
    gathered = gather_block(
        query_weight,
        key_weight,
        value_weight,
        gate_weight,
        rate_weight,
        output_weight,
        ffn_gate,
        ffn_up,
        ffn_down,
    )
    w_query, w_key, w_value, w_gate, w_rate, w_output, w_ffgate, w_ffup, w_ffdown = gathered
    cotangent = upstream.reshape(row_count, model_width)
    product_grad = back_dot(cotangent, w_ffdown)
    grad_down = weight_dot(product, cotangent)
    gate_grad_full, up_grad_full = swiglu_back(product_grad)
    gate_grad = gate_grad_full.astype(jnp.bfloat16)
    up_grad = up_grad_full.astype(jnp.bfloat16)
    normed_two_grad = back_dot(gate_grad, w_ffgate) + back_dot(up_grad, w_ffup)
    grad_ffgate = weight_dot(normed_two, gate_grad)
    grad_ffup = weight_dot(normed_two, up_grad)
    hidden_part, ffn_gain_grad = norm_two_back(normed_two_grad)
    hidden_grad = cotangent.astype(jnp.float32) + hidden_part
    branch_grad = hidden_grad.astype(jnp.bfloat16)
    gated_grad = back_dot(branch_grad, w_output)
    grad_output = weight_dot(gated, branch_grad)
    mixture_grad_rows, gate_pre_grad, out_gain_grad = gate_back(
        gated_grad.reshape(batch_count, segment_len, value_width)
    )
    mixture_grad = mixture_grad_rows.transpose(0, 2, 1, 3)
    local_term = batch_apply(carried, mixture_grad, "shtk,shtv->shkv")
    flipped = mapping.transpose(0, 1, 3, 2)
    leaving = jnp.zeros_like(offset)
    for hop_index in range(lax.axis_size("seq") - 1):
        leaving = passed_along(
            batch_apply(flipped, leaving, "shij,shjk->shik") + local_term, "seq", -1
        )
    carried_grad = batch_apply(mixture_grad, entering, "shtv,shkv->shtk")
    mapping_grad = batch_apply(leaving, entering, "shkv,shjv->shkj")
    query_grad, key_grad, value_grad, beta_grad, decay_grad = seg_back(
        (mixture_grad, carried_grad, mapping_grad, leaving)
    )
    ext_grads = prep_back(
        (
            round_trip(query_grad).transpose(0, 2, 1, 3),
            round_trip(key_grad).transpose(0, 2, 1, 3),
            round_trip(value_grad).transpose(0, 2, 1, 3),
            beta_grad.transpose(0, 2, 1),
            decay_grad.transpose(0, 2, 1),
        )
    )
    (
        query_ext_grad,
        key_ext_grad,
        value_ext_grad,
        rate_grad_full,
        conv_grad,
        decay_log_grad,
        decay_bias_grad,
    ) = ext_grads
    returned = (
        passed_along(query_ext_grad[:, :conv_lead].astype(jnp.bfloat16), "seq", -1).astype(
            jnp.float32
        ),
        passed_along(key_ext_grad[:, :conv_lead].astype(jnp.bfloat16), "seq", -1).astype(
            jnp.float32
        ),
        passed_along(value_ext_grad[:, :conv_lead].astype(jnp.bfloat16), "seq", -1).astype(
            jnp.float32
        ),
    )

    def settle(ext_grad, incoming, channels):
        own_rows = ext_grad[:, conv_lead:]
        own_rows = jnp.concatenate(
            [
                own_rows[:, : segment_len - conv_lead],
                own_rows[:, segment_len - conv_lead :] + incoming,
            ],
            axis=1,
        )
        return own_rows.reshape(row_count, channels).astype(jnp.bfloat16)

    query_pre_grad = settle(query_ext_grad, returned[0], key_width)
    key_pre_grad = settle(key_ext_grad, returned[1], key_width)
    value_pre_grad = settle(value_ext_grad, returned[2], value_width)
    gate_pre_rounded = gate_pre_grad.reshape(row_count, value_width).astype(jnp.bfloat16)
    rate_grad = rate_grad_full.reshape(row_count, -1).astype(jnp.bfloat16)
    normed_grad = (
        back_dot(query_pre_grad, w_query)
        + back_dot(key_pre_grad, w_key)
        + back_dot(value_pre_grad, w_value)
        + back_dot(gate_pre_rounded, w_gate)
        + back_dot(rate_grad, w_rate)
    )
    grad_query = weight_dot(normed, query_pre_grad)
    grad_key = weight_dot(normed, key_pre_grad)
    grad_value = weight_dot(normed, value_pre_grad)
    grad_gate = weight_dot(normed, gate_pre_rounded)
    grad_rate = weight_dot(normed, rate_grad)
    token_part, norm_gain_grad = norm_back(normed_grad)
    input_grad = (hidden_grad + token_part).reshape(inputs.shape)
    summed = sum_block(
        grad_query,
        grad_key,
        grad_value,
        grad_gate,
        grad_rate,
        grad_output,
        grad_ffgate,
        grad_ffup,
        grad_down,
    )
    small_sums = lax.psum(
        (norm_gain_grad, conv_grad, decay_log_grad, decay_bias_grad, out_gain_grad, ffn_gain_grad),
        ("dp", "seq"),
    )
    return (
        outputs,
        input_grad,
        small_sums[0],
        summed[0],
        summed[1],
        summed[2],
        summed[3],
        summed[4],
        small_sums[1],
        small_sums[2],
        small_sums[3],
        small_sums[4],
        summed[5],
        small_sums[5],
        summed[6],
        summed[7],
        summed[8],
    )


def solution(mesh):
    in_specs = (
        P(None, "dp", "seq", None),
        P(None, "dp", "seq", None),
        P(),
        P("dp", "seq"),
        P("dp", "seq"),
        P("dp", "seq"),
        P("dp", "seq"),
        P("dp", "seq"),
        P(),
        P(),
        P(),
        P(),
        P("dp", "seq"),
        P(),
        P("dp", "seq"),
        P("dp", "seq"),
        P("dp", "seq"),
    )
    out_specs = (
        P(None, "dp", "seq", None),
        P(None, "dp", "seq", None),
        P(),
        P("dp", "seq"),
        P("dp", "seq"),
        P("dp", "seq"),
        P("dp", "seq"),
        P("dp", "seq"),
        P(),
        P(),
        P(),
        P(),
        P("dp", "seq"),
        P(),
        P("dp", "seq"),
        P("dp", "seq"),
        P("dp", "seq"),
    )
    return jax.shard_map(shards, mesh=mesh, in_specs=in_specs, out_specs=out_specs, check_vma=False)
```

profile of v0, /device:TPU:0, one launch (start us, length us, event | category | flops | bytes accessed | tf_op | source)
XLA Modules:
  0.0 2679.2 jit_solution(6936189617625613170)
XLA Ops:
  7.3 17.6 all_gather.74
  25.0 15.0 all_gather.78
  40.0 17.3 all_gather.76
  57.4 16.7 all_gather.80
  74.2 16.6 all_gather.82
  91.0 19.0 all_gather.84
  110.1 16.1 all_gather.86
  258.5 356.7 %while.137 = (s32[]{:T(128)}, f32[3,8,128,128]{3,2,1,0:T(8,128)}, f32[3,8,128,256]{3,2,1,0:T(8,128)S(1)}, f32[4,3,8,64,256]{4,3,2,1,0:T(8,128)}, f32[4,3,8,64,12...) while((s32[]{:T(128)}, f32[3,8,128,128]{3,2,1,0:T(8,128)}, ...), condition=%wide.region_5.6_spmd.clone.clone.clone, body=%wide.region_3.5_spmd.clone.clone.sunk.clone | while | flops 4693044224 | bytes 135315408 | solution.py:152
  620.6 66.9 %collective-permute-done.3 = f32[3,8,128,256]{3,2,1,0:T(8,128)S(1)} collective-permute-done((f32[3,8,128,256]{3,2,1,0:T(8,128)S(1)}, f32[3,8,128,256]{3,2,1,0:T(8,128)S(1)}, u32[]{:S(2)}, u32[]{:S(2)}) %collective-permute-start.3) | collective-permute-done | bytes 3145760 | tf_op jit(solution)/shard_map/ppermute | solution.py:15
  699.6 80.7 %all_gather.88 = bf16[352,1024]{1,0:T(8,128)(2,1)} all-gather(bf16[352,256]{1,0:T(8,128)(2,1)S(1)} %copy-done.96), channel_id=1, replica_groups=mesh['dp'=8,'seq'=4] {'seq'}, dimensions={1}, use_global_device_ids=true | all-gather | bytes 901120 | tf_op jit(solution)/shard_map/all_gather | solution.py:180
  801.8 50.7 %collective-permute-done.5 = f32[3,8,128,256]{3,2,1,0:T(8,128)S(1)} collective-permute-done((f32[3,8,128,256]{3,2,1,0:T(8,128)}, f32[3,8,128,256]{3,2,1,0:T(8,128)S(1)}, u32[]{:S(2)}, u32[]{:S(2)}) %collective-permute-start.5) | collective-permute-done | bytes 3145760 | tf_op jit(solution)/shard_map/ppermute | solution.py:15
  899.5 15.2 multiply_convert_fusion
  973.3 63.7 %collective-permute-done.6 = f32[3,8,128,256]{3,2,1,0:T(8,128)S(1)} collective-permute-done((f32[3,8,128,256]{3,2,1,0:T(8,128)S(1)}, f32[3,8,128,256]{3,2,1,0:T(8,128)S(1)}, u32[]{:S(2)}, u32[]{:S(2)}) %collective-permute-start.6) | collective-permute-done | bytes 3145760 | tf_op jit(solution)/shard_map/ppermute | solution.py:15
  1042.6 62.4 %collective-permute-done.7 = f32[3,8,128,256]{3,2,1,0:T(8,128)S(1)} collective-permute-done((f32[3,8,128,256]{3,2,1,0:T(8,128)S(1)}, f32[3,8,128,256]{3,2,1,0:T(8,128)S(1)}, u32[]{:S(2)}, u32[]{:S(2)}) %collective-permute-start.7) | collective-permute-done | bytes 3145760 | tf_op jit(solution)/shard_map/ppermute | solution.py:15
  1136.4 38.3 %collective-permute-done.8 = f32[3,8,128,256]{3,2,1,0:T(8,128)S(1)} collective-permute-done((f32[3,8,128,256]{3,2,1,0:T(8,128)}, f32[3,8,128,256]{3,2,1,0:T(8,128)S(1)}, u32[]{:S(2)}, u32[]{:S(2)}) %collective-permute-start.8) | collective-permute-done | bytes 3145760 | tf_op jit(solution)/shard_map/ppermute | solution.py:15
  1183.2 595.5 %while.136 = (s32[]{:T(128)}, f32[3,8,128,128]{3,2,1,0:T(8,128)}, f32[3,8,128,256]{3,2,1,0:T(8,128)S(1)}, bf16[4,3,8,64,128]{4,3,0,2,1:T(8,128)(2,1)}, bf16[4,3,...) while((s32[]{:T(128)}, f32[3,8,128,128]{3,2,1,0:T(8,128)}, ...), condition=%wide.region_23.24_spmd.clone.clone.clone, body=%wide.region_10.23_spmd.clone.clone.sunk.clone | while | flops 9378605056 | bytes 346784192 | solution.py:152
  1912.5 20.0 multiply_reduce_fusion.4
  1941.3 13.1 pad_add_fusion
  1991.6 27.5 %reduce-scatter.46.cloned.1.call-done = f32[128,2816]{1,0:T(8,128)} async-done(((f32[1024,2816]{1,0:T(8,128)}), f32[128,2816]{1,0:T(8,128)}) %reduce-scatter.46.cloned.1.call-update) | async-done | bytes 1441808 | tf_op jit(solution)/shard_map/reduce_scatter | solution.py:214
  2022.1 87.2 %reduce-scatter.44.cloned.1.call-done = f32[128,2816]{1,0:T(8,128)} async-done(((f32[1024,2816]{1,0:T(8,128)}), f32[128,2816]{1,0:T(8,128)}) %reduce-scatter.44.cloned.1.call-update) | async-done | bytes 1441808 | tf_op jit(solution)/shard_map/reduce_scatter | solution.py:213
  2113.6 85.9 %reduce-scatter.48.cloned.1.call-done = f32[352,1024]{1,0:T(8,128)} async-done(((f32[2816,1024]{1,0:T(8,128)}), f32[352,1024]{1,0:T(8,128)}) %reduce-scatter.48.cloned.1.call-update) | async-done | bytes 1441808 | tf_op jit(solution)/shard_map/reduce_scatter | solution.py:215
  2226.3 47.8 %reduce-scatter.30.cloned.1.call-done = f32[128,2048]{1,0:T(8,128)} async-done(((f32[1024,2048]{1,0:T(8,128)}), f32[128,2048]{1,0:T(8,128)}) %reduce-scatter.30.cloned.1.call-update) | async-done | bytes 1048592 | tf_op jit(solution)/shard_map/reduce_scatter | solution.py:209
  2284.0 39.5 %all-reduce.33 = (f32[1024]{0:T(1024)}, f32[8]{0:T(128)}, f32[8]{0:T(128)}, f32[256]{0:T(256)}, f32[1024]{0:T(1024)}) all-reduce(f32[1024]{0:T(1024)S(1)} %get-tuple-element.3216, f32[8]{0:T(128)S(1)} %negate_multiply_fusion, f32[8]{0:T(128)S(1)} %get-tuple-element.3436, ...), channel_id=1, replica_groups=mesh['dp'=8,'seq'=4] {'dp','seq'}, use_global_device_ids=true, to_apply=%region_28.29 | all-reduce | flops 2320 | bytes 18560 | tf_op jit(solution)/shard_map/psum | solution.py:453
  2340.3 92.0 %all-reduce.36.cloned.1.call-done = f32[4,4096]{1,0:T(4,128)} async-done(((f32[4,4096]{1,0:T(4,128)}), f32[4,4096]{1,0:T(4,128)}) %all-reduce.36.cloned.1.call-update) | async-done | bytes 65552 | tf_op jit(solution)/shard_map/psum | solution.py:453
  2432.3 30.9 %reduce-scatter.42.cloned.1.call-done = f32[256,256]{1,0:T(8,128)} async-done(((f32[256,1024]{1,0:T(8,128)}), f32[256,256]{1,0:T(8,128)}) %reduce-scatter.42.cloned.1.call-update) | async-done | bytes 262160 | tf_op jit(solution)/shard_map/reduce_scatter | solution.py:223
  2463.2 28.6 %reduce-scatter.36.cloned.1.call-done = f32[128,512]{1,0:T(8,128)} async-done(((f32[128,2048]{1,0:T(8,128)}), f32[128,512]{1,0:T(8,128)}) %reduce-scatter.36.cloned.1.call-update) | async-done | bytes 262160 | tf_op jit(solution)/shard_map/reduce_scatter | solution.py:221
  2491.8 23.2 reduce-scatter.28.cloned.1.call-done
  2515.0 22.8 reduce-scatter.24.cloned.1.call-done
  2537.7 34.5 %reduce-scatter.54.cloned.1.call-done = f32[704,128]{1,0:T(8,128)} async-done(((f32[2816,128]{1,0:T(8,128)}), f32[704,128]{1,0:T(8,128)}) %reduce-scatter.54.cloned.1.call-update) | async-done | bytes 360464
  2572.2 34.9 %reduce-scatter.52.cloned.1.call-done = f32[704,128]{1,0:T(8,128)} async-done(((f32[2816,128]{1,0:T(8,128)}), f32[704,128]{1,0:T(8,128)}) %reduce-scatter.52.cloned.1.call-update) | async-done | bytes 360464
  2607.2 35.1 %reduce-scatter.50.cloned.1.call-done = f32[352,256]{1,0:T(8,128)} async-done(((f32[352,1024]{1,0:T(8,128)}), f32[352,256]{1,0:T(8,128)}) %reduce-scatter.50.cloned.1.call-update) | async-done | bytes 360464 | tf_op jit(solution)/shard_map/reduce_scatter | solution.py:226
  2642.2 28.8 %reduce-scatter.32.cloned.1.call-done = f32[128,512]{1,0:T(8,128)} async-done(((f32[128,2048]{1,0:T(8,128)}), f32[128,512]{1,0:T(8,128)}) %reduce-scatter.32.cloned.1.call-update) | async-done | bytes 262160 | tf_op jit(solution)/shard_map/reduce_scatter | solution.py:220
  (1216 shorter events, 1473.0 us)
Async XLA Ops:
  7.2 146.0 %all-gather.10.cloned.1.call-start = ((), (), s32[]{:S(2)}) async-start(), calls=%async_computation.17 | async-start | bytes 2359296 | tf_op jit(solution)/shard_map/all_gather | solution.py:184
  24.9 134.8 %all-gather.14.cloned.1.call-start = ((), (), s32[]{:S(2)}) async-start(), calls=%async_computation.19 | async-start | bytes 2359296 | tf_op jit(solution)/shard_map/all_gather | solution.py:183
  40.0 153.5 %all-gather.12.cloned.1.call-start = ((), (), s32[]{:S(2)}) async-start(), calls=%async_computation.18 | async-start | bytes 4718592 | tf_op jit(solution)/shard_map/all_gather | solution.py:185
  57.4 734.5 %all-gather.16.cloned.1.call-start = ((), (), s32[]{:S(2)}) async-start(), calls=%async_computation.20 | async-start | bytes 4718592 | tf_op jit(solution)/shard_map/all_gather | solution.py:186
  74.2 796.5 %all-gather.18.cloned.1.call-start = ((), (), s32[]{:S(2)}) async-start(), calls=%async_computation.21 | async-start | bytes 4718592 | tf_op jit(solution)/shard_map/all_gather | solution.py:188
  90.9 788.6 %all-gather.20.cloned.1.call-start = ((), (), s32[]{:S(2)}) async-start(), calls=%async_computation.22 | async-start | bytes 6488064 | tf_op jit(solution)/shard_map/all_gather | solution.py:189
  110.0 779.7 %all-gather.22.cloned.1.call-start = ((), (), s32[]{:S(2)}) async-start(), calls=%async_computation.23 | async-start | bytes 6488064 | tf_op jit(solution)/shard_map/all_gather | solution.py:190
  126.2 773.2 %all-gather.24.cloned.1.call-start = ((), (), s32[]{:S(2)}) async-start(), calls=%async_computation.24 | async-start | bytes 6488064 | tf_op jit(solution)/shard_map/all_gather | solution.py:191
  618.4 69.1 %collective-permute-start.3 = (f32[3,8,128,256]{3,2,1,0:T(8,128)S(1)}, f32[3,8,128,256]{3,2,1,0:T(8,128)S(1)}, u32[]{:S(2)}, u32[]{:S(2)}) collective-permute-start(f32[3,8,128,256]{3,2,1,0:T(8,128)S(1)} %convolution_add_fusion.20), channel_id=1, source_target_pairs={{0,1},{1,2},{2,3},{4,5},{5,6},{6,7},{8,9},{9,10},{10,11},{12,13},{... | collective-permute-start | bytes 9437192 | tf_op jit(solution)/shard_map/ppermute | solution.py:15
  693.4 87.1 %collective-permute-start.4 = (f32[3,8,128,256]{3,2,1,0:T(8,128)}, f32[3,8,128,256]{3,2,1,0:T(8,128)}, u32[]{:S(2)}, u32[]{:S(2)}) collective-permute-start(f32[3,8,128,256]{3,2,1,0:T(8,128)} %convolution_add_fusion.19), channel_id=1, source_target_pairs={{0,1},{1,2},{2,3},{4,5},{5,6},{6,7},{8,9},{9,10},{10,11},{12,13},{... | collective-permute-start | bytes 9437192 | tf_op jit(solution)/shard_map/ppermute | solution.py:15
  780.4 1208.4 %reduce-scatter.40.cloned.1.call-start = ((), (), s32[]{:S(2)}) async-start(), calls=%async_computation.35 | async-start | bytes 9437184 | tf_op jit(solution)/shard_map/reduce_scatter | solution.py:212
  787.5 65.1 %collective-permute-start.5 = (f32[3,8,128,256]{3,2,1,0:T(8,128)}, f32[3,8,128,256]{3,2,1,0:T(8,128)S(1)}, u32[]{:S(2)}, u32[]{:S(2)}) collective-permute-start(f32[3,8,128,256]{3,2,1,0:T(8,128)} %convolution_add_fusion.18), channel_id=1, source_target_pairs={{0,1},{1,2},{2,3},{4,5},{5,6},{6,7},{8,9},{9,10},{10,11},{12,13},{... | collective-permute-start | bytes 9437192 | tf_op jit(solution)/shard_map/ppermute | solution.py:15
  937.2 1052.4 %reduce-scatter.34.cloned.1.call-start = ((), (), s32[]{:S(2)}) async-start(), calls=%async_computation.31 | async-start | bytes 9437184 | tf_op jit(solution)/shard_map/reduce_scatter | solution.py:210
  972.0 65.0 %collective-permute-start.6 = (f32[3,8,128,256]{3,2,1,0:T(8,128)S(1)}, f32[3,8,128,256]{3,2,1,0:T(8,128)S(1)}, u32[]{:S(2)}, u32[]{:S(2)}) collective-permute-start(f32[3,8,128,256]{3,2,1,0:T(8,128)S(1)} %convolution_add_fusion.17), channel_id=1, source_target_pairs={{1,0},{2,1},{3,2},{5,4},{6,5},{7,6},{9,8},{10,9},{11,10},{13,12},{... | collective-permute-start | bytes 9437192 | tf_op jit(solution)/shard_map/ppermute | solution.py:15
  1041.3 63.7 %collective-permute-start.7 = (f32[3,8,128,256]{3,2,1,0:T(8,128)S(1)}, f32[3,8,128,256]{3,2,1,0:T(8,128)S(1)}, u32[]{:S(2)}, u32[]{:S(2)}) collective-permute-start(f32[3,8,128,256]{3,2,1,0:T(8,128)S(1)} %convolution_add_fusion.16), channel_id=1, source_target_pairs={{1,0},{2,1},{3,2},{5,4},{6,5},{7,6},{9,8},{10,9},{11,10},{13,12},{... | collective-permute-start | bytes 9437192 | tf_op jit(solution)/shard_map/ppermute | solution.py:15
  1111.0 63.7 %collective-permute-start.8 = (f32[3,8,128,256]{3,2,1,0:T(8,128)}, f32[3,8,128,256]{3,2,1,0:T(8,128)S(1)}, u32[]{:S(2)}, u32[]{:S(2)}) collective-permute-start(f32[3,8,128,256]{3,2,1,0:T(8,128)} %convolution_add_fusion.15), channel_id=1, source_target_pairs={{1,0},{2,1},{3,2},{5,4},{6,5},{7,6},{9,8},{10,9},{11,10},{13,12},{... | collective-permute-start | bytes 9437192 | tf_op jit(solution)/shard_map/ppermute | solution.py:15
  1136.1 854.1 %reduce-scatter.26.cloned.1.call-start = ((), (), s32[]{:S(2)}) async-start(), calls=%async_computation.27 | async-start | bytes 4718592 | tf_op jit(solution)/shard_map/reduce_scatter | solution.py:208
  1822.4 168.5 %reduce-scatter.22.cloned.1.call-start = ((), (), s32[]{:S(2)}) async-start(), calls=%async_computation.25 | async-start | bytes 4718592 | tf_op jit(solution)/shard_map/reduce_scatter | solution.py:207
  1867.9 151.2 %reduce-scatter.46.cloned.1.call-start = ((), (), s32[]{:S(2)}) async-start(), calls=%async_computation.38 | async-start | bytes 12976128 | tf_op jit(solution)/shard_map/reduce_scatter | solution.py:214
  1879.0 230.4 %reduce-scatter.44.cloned.1.call-start = ((), (), s32[]{:S(2)}) async-start(), calls=%async_computation.37 | async-start | bytes 12976128 | tf_op jit(solution)/shard_map/reduce_scatter | solution.py:213
  1888.9 310.6 %reduce-scatter.48.cloned.1.call-start = ((), (), s32[]{:S(2)}) async-start(), calls=%async_computation.39 | async-start | bytes 12976128 | tf_op jit(solution)/shard_map/reduce_scatter | solution.py:215
  1900.3 373.8 %reduce-scatter.30.cloned.1.call-start = ((), (), s32[]{:S(2)}) async-start(), calls=%async_computation.29 | async-start | bytes 9437184 | tf_op jit(solution)/shard_map/reduce_scatter | solution.py:209
  1985.9 342.9 %reduce-scatter.38.cloned.1.call-start = ((), (), s32[]{:S(2)}) async-start(), calls=%async_computation.33 | async-start | bytes 73728 | tf_op jit(solution)/shard_map/reduce_scatter | solution.py:211
  1987.9 444.4 %all-reduce.36.cloned.1.call-start = ((), (), s32[]{:S(2)}) async-start(), calls=%async_computation.34 | async-start | bytes 131072 | tf_op jit(solution)/shard_map/psum | solution.py:453
  1988.8 474.4 %reduce-scatter.42.cloned.1.call-start = ((), (), s32[]{:S(2)}) async-start(), calls=%async_computation.36 | async-start | bytes 1310720 | tf_op jit(solution)/shard_map/reduce_scatter | solution.py:223
  1989.5 502.3 %reduce-scatter.36.cloned.1.call-start = ((), (), s32[]{:S(2)}) async-start(), calls=%async_computation.32 | async-start | bytes 1310720 | tf_op jit(solution)/shard_map/reduce_scatter | solution.py:221
  1990.1 524.9 %reduce-scatter.28.cloned.1.call-start = ((), (), s32[]{:S(2)}) async-start(), calls=%async_computation.28 | async-start | bytes 655360 | tf_op jit(solution)/shard_map/reduce_scatter | solution.py:219
  1990.8 546.9 %reduce-scatter.24.cloned.1.call-start = ((), (), s32[]{:S(2)}) async-start(), calls=%async_computation.26 | async-start | bytes 655360 | tf_op jit(solution)/shard_map/reduce_scatter | solution.py:218
  1991.6 580.7 %reduce-scatter.54.cloned.1.call-start = ((), (), s32[]{:S(2)}) async-start(), calls=%async_computation.42 | async-start | bytes 1802240
  2022.1 585.1 %reduce-scatter.52.cloned.1.call-start = ((), (), s32[]{:S(2)}) async-start(), calls=%async_computation.41 | async-start | bytes 1802240
  2112.3 529.9 %reduce-scatter.50.cloned.1.call-start = ((), (), s32[]{:S(2)}) async-start(), calls=%async_computation.40 | async-start | bytes 1802240 | tf_op jit(solution)/shard_map/reduce_scatter | solution.py:226
  2199.5 471.4 %reduce-scatter.32.cloned.1.call-start = ((), (), s32[]{:S(2)}) async-start(), calls=%async_computation.30 | async-start | bytes 1310720 | tf_op jit(solution)/shard_map/reduce_scatter | solution.py:220
  (266 other events, 2948.2 us)
Sparse Core Ops, SparseCore 0:
  25.0 27.9 all-gather.9
  54.9 27.8 all-gather.13
  84.7 36.7 all-gather.11
  123.2 36.7 all-gather.15
  161.7 36.6 all-gather.17
  200.2 44.3 all-gather.19
  246.4 44.3 all-gather.21
  780.5 43.0 all-gather.23
  937.3 72.8 reduce-scatter.39
  1136.2 73.3 reduce-scatter.33
  1822.5 51.3 reduce-scatter.25
  1877.5 51.2 reduce-scatter.21
  1932.3 86.7 reduce-scatter.45
  2022.5 86.7 reduce-scatter.43
  2112.7 86.7 reduce-scatter.47
  2202.8 71.2 reduce-scatter.29
  2277.8 31.4 reduce-scatter.37
  2314.7 117.5 all-reduce.35
  2435.2 27.9 reduce-scatter.41
  2466.0 25.7 reduce-scatter.35
  2494.7 20.2 reduce-scatter.27
  2517.8 19.8 reduce-scatter.23
  2540.6 31.5 reduce-scatter.53
  2575.0 32.1 reduce-scatter.51
  2610.0 32.1 reduce-scatter.49
  2644.9 26.0 reduce-scatter.31
where the time goes:
time: 2690 us; the launch traced here: 2680 us
  matrix products  1050 us (39%)
  waiting for transfers between devices  867 us (32%)
  blocking collectives  269 us (10%)
  other arithmetic  223 us (8%)
  local copies, waits for them, and re-layouts  188 us (7%)
  loops' own time  40.7 us (2%)
  starting transfers between devices  28.5 us (1%)
    dot_general x264, matrix products, high_dot(): jnp.dot(left_mat, right_mat, precision=lax.Precision.HIGHEST, preferred_e...  814 us
    ppermute x12, waiting for transfers between devices, passed_along(): return lax.ppermute(block, axis, route)  285 us
    psum x1, waiting for transfers between devices, shards(): lax.psum((norm_gain_grad, conv_grad, decay_log_grad, decay_bias_grad, out...  92 us
    reduce_scatter x1, waiting for transfers between devices, sum_block(): lax.psum_scatter(grad_ffgate, 'dp', scatter_dimension=0, tiled=True)  87.2 us
    reduce_scatter x1, waiting for transfers between devices, sum_block(): lax.psum_scatter(grad_down, 'dp', scatter_dimension=0, tiled=True)  85.9 us
    all_gather x1, blocking collectives, gather_block(): lax.all_gather(ffn_down, 'seq', axis=1, tiled=True)  80.7 us
    unnamed x28, waiting for transfers between devices  72.3 us
    dot_general x9, matrix products, plain_dot(): return jnp.dot(left_mat, right_mat, preferred_element_type=jnp.float32)  60.4 us
  transfers between devices with their start and end apart: 38, of which 20 were waited for; matrix products, arithmetic and copies ran while one was open for 52% of the time, Pallas kernels for 0%

commit v1 on v0

v1 whole, which is shorter than its diff:
```python
import jax
import jax.numpy as jnp
from jax import lax
from jax.sharding import PartitionSpec as P

GROUP = 64


EPSILON = 1e-06


def passed_along(block, axis, distance):
    devices = range(lax.axis_size(axis))
    route = [(i - distance, i) for i in devices if i - distance in devices]
    return lax.ppermute(block, axis, route)


def plain_dot(left_mat, right_mat):
    return jnp.dot(left_mat, right_mat, preferred_element_type=jnp.float32)


def back_dot(left_mat, right_mat):
    return lax.dot_general(
        left_mat, right_mat, (((1,), (1,)), ((), ())), preferred_element_type=jnp.float32
    )


def weight_dot(left_mat, right_mat):
    return lax.dot_general(
        left_mat, right_mat, (((0,), (0,)), ((), ())), preferred_element_type=jnp.float32
    )


def mid_dot(left_mat, right_mat, formula):
    return jnp.einsum(formula, left_mat, right_mat, precision=lax.Precision.HIGH)


def rms_scale(values, gain_vec):
    return (
        values * lax.rsqrt(jnp.mean(values * values, axis=-1, keepdims=True) + EPSILON) * gain_vec
    )


def swiglu_product(gate_vals, up_vals):
    return jax.nn.silu(gate_vals) * up_vals


def gate_output(mixture, gate_pre, out_gain):
    head_count = mixture.shape[-2]
    gated_rows = rms_scale(mixture, out_gain) * jax.nn.silu(
        gate_pre.reshape(gate_pre.shape[:-1] + (head_count, -1))
    )
    return gated_rows.reshape(gate_pre.shape)


def prepare(query_ext, key_ext, value_ext, rate_pre, conv_weight, decay_log, decay_bias):
    conv_lead = conv_weight.shape[0] - 1
    length = query_ext.shape[1] - conv_lead
    head_count = decay_log.shape[0]
    query_width = query_ext.shape[2]
    key_dim = query_width // head_count
    batch_size = query_ext.shape[0]

    def convolve(extended, kernel):
        summed_taps = kernel[0] * extended[:, 0:length]
        for offset_idx in range(1, conv_lead + 1):
            summed_taps = (
                summed_taps + kernel[offset_idx] * extended[:, offset_idx : offset_idx + length]
            )
        return jax.nn.silu(summed_taps)

    queries = convolve(query_ext, conv_weight[:, :query_width]).reshape(
        batch_size, length, head_count, key_dim
    )
    key_rows = convolve(key_ext, conv_weight[:, query_width : 2 * query_width]).reshape(
        batch_size, length, head_count, key_dim
    )
    values = convolve(value_ext, conv_weight[:, 2 * query_width :]).reshape(
        batch_size, length, head_count, -1
    )
    queries = (
        queries
        * lax.rsqrt(jnp.sum(queries * queries, axis=-1, keepdims=True) + EPSILON)
        * key_dim ** (-0.5)
    )
    key_rows = key_rows * lax.rsqrt(jnp.sum(key_rows * key_rows, axis=-1, keepdims=True) + EPSILON)
    beta_rows = jax.nn.sigmoid(rate_pre[..., head_count:])
    decays = -jnp.exp(decay_log) * jax.nn.softplus(rate_pre[..., :head_count] + decay_bias)
    return (queries, key_rows, values, beta_rows, decays)


@jax.custom_vjp
def unit_inverse(mixing):
    size = mixing.shape[-1]
    row_index = lax.broadcasted_iota(jnp.int32, (size, size), 0)
    col_index = lax.broadcasted_iota(jnp.int32, (size, size), 1)

    def between(width):
        same = row_index // (2 * width) == col_index // (2 * width)
        return same & (row_index // width > col_index // width)

    inverse = jnp.eye(size, dtype=jnp.float32) - jnp.where(between(1), mixing, 0.0)
    width = 2
    while width < size:
        linked = jnp.where(between(width), mixing, 0.0)
        inverse = inverse - mid_dot(
            mid_dot(inverse, linked, "...ij,...jk->...ik"), inverse, "...ij,...jk->...ik"
        )
        width = width * 2
    return inverse


def unit_inverse_keep(mixing):
    inverse = unit_inverse(mixing)
    return inverse, inverse


def unit_inverse_back(inverse, grad):
    partial = mid_dot(inverse, grad, "...ji,...jk->...ik")
    return (-mid_dot(partial, inverse, "...ij,...kj->...ik"),)


unit_inverse.defvjp(unit_inverse_keep, unit_inverse_back)


def group_maps(queries, key_rows, values, beta_rows, decays):
    group_len = decays.shape[-1]
    key_dim = key_rows.shape[-1]
    row_index = lax.broadcasted_iota(jnp.int32, (group_len, group_len), 0)
    col_index = lax.broadcasted_iota(jnp.int32, (group_len, group_len), 1)
    strict_lower = row_index > col_index
    lower_incl = row_index >= col_index
    cumulative = jnp.sum(jnp.where(lower_incl, decays[..., None, :], 0.0), axis=-1)
    decay_ratio = jnp.exp(
        jnp.where(lower_incl, cumulative[..., :, None] - cumulative[..., None, :], 0.0)
    )
    overlaps = jnp.einsum("...ik,...jk->...ij", key_rows, key_rows)
    mixing = jnp.where(strict_lower, beta_rows[..., :, None] * overlaps * decay_ratio, 0.0)
    solved = unit_inverse(mixing) * beta_rows[..., None, :]
    growth = jnp.exp(cumulative)[..., None]
    wy_keys = mid_dot(solved, growth * key_rows, "...ij,...jk->...ik")
    wy_values = mid_dot(solved, values, "...ij,...jk->...ik")
    matches = jnp.einsum("...ik,...jk->...ij", queries, key_rows)
    scores = jnp.where(lower_incl, matches * decay_ratio, 0.0)
    tail_keys = jnp.exp(cumulative[..., -1:] - cumulative)[..., None] * key_rows
    step_map = growth[..., -1:, :] * jnp.eye(key_dim, dtype=jnp.float32) - mid_dot(
        tail_keys, wy_keys, "...tk,...tj->...kj"
    )
    step_offset = mid_dot(tail_keys, wy_values, "...tk,...tv->...kv")
    read_map = growth * queries - mid_dot(scores, wy_keys, "...ij,...jk->...ik")
    read_offset = mid_dot(scores, wy_values, "...ij,...jk->...ik")
    return (step_map, step_offset, read_map, read_offset)


def round_trip(values):
    return values.astype(jnp.bfloat16).astype(jnp.float32)


def gather_block(matrices):
    wide = [0, 1, 2, 3, 4, 6, 7]
    tall = [5, 8]
    wide_all = lax.all_gather(jnp.concatenate([matrices[i] for i in wide], axis=1), "seq")
    tall_all = lax.all_gather(jnp.concatenate([matrices[i] for i in tall], axis=0), "seq")
    rows = {}
    start = 0
    for i in wide:
        stop = start + matrices[i].shape[1]
        rows[i] = wide_all[:, :, start:stop]
        start = stop
    start = 0
    for i in tall:
        stop = start + matrices[i].shape[0]
        rows[i] = tall_all[:, start:stop]
        start = stop
    return tuple(
        lax.all_gather(
            rows[i].transpose(1, 0, 2).reshape(matrices[i].shape[0], -1), "dp", axis=0, tiled=True
        )
        for i in range(len(matrices))
    )


def row_sum(grad):
    return lax.psum_scatter(
        grad.astype(jnp.bfloat16), "dp", scatter_dimension=0, tiled=True
    )


def column_sums(grads):
    wide = [0, 1, 2, 3, 4, 6, 7]
    tall = [5, 8]
    parts = lax.axis_size("seq")
    split = [g.reshape(g.shape[0], parts, -1).transpose(1, 0, 2) for g in grads]
    wide_sum = lax.psum_scatter(
        jnp.concatenate([split[i] for i in wide], axis=2), "seq", scatter_dimension=0
    )
    tall_sum = lax.psum_scatter(
        jnp.concatenate([split[i] for i in tall], axis=1), "seq", scatter_dimension=0
    )
    found = {}
    start = 0
    for i in wide:
        stop = start + split[i].shape[2]
        found[i] = wide_sum[:, start:stop].astype(jnp.float32)
        start = stop
    start = 0
    for i in tall:
        stop = start + split[i].shape[1]
        found[i] = tall_sum[start:stop].astype(jnp.float32)
        start = stop
    return tuple(found[i] for i in range(len(grads)))


def hop_sum(block, axis_distance):
    return passed_along(block.astype(jnp.bfloat16), "seq", axis_distance).astype(jnp.float32)


def shards(
    inputs,
    upstream,
    norm_gain,
    query_weight,
    key_weight,
    value_weight,
    gate_weight,
    rate_weight,
    conv_weight,
    decay_log,
    decay_bias,
    out_gain,
    output_weight,
    ffn_gain,
    ffn_gate,
    ffn_up,
    ffn_down,
):
    batch_count = inputs.shape[0] * inputs.shape[1]
    segment_len = inputs.shape[2]
    model_width = inputs.shape[3]
    row_count = batch_count * segment_len
    conv_lead = conv_weight.shape[0] - 1
    key_width = query_weight.shape[1] * lax.axis_size("seq")
    value_width = value_weight.shape[1] * lax.axis_size("seq")
    tokens = inputs.reshape(row_count, model_width).astype(jnp.float32)
    gathered = gather_block((
        query_weight,
        key_weight,
        value_weight,
        gate_weight,
        rate_weight,
        output_weight,
        ffn_gate,
        ffn_up,
        ffn_down,
    ))
    w_query, w_key, w_value, w_gate, w_rate, w_output, w_ffgate, w_ffup, w_ffdown = gathered
    normed_full, norm_back = jax.vjp(rms_scale, tokens, norm_gain)
    normed = normed_full.astype(jnp.bfloat16)
    query_pre = (
        plain_dot(normed, w_query).astype(jnp.bfloat16).reshape(batch_count, segment_len, key_width)
    )
    key_pre = (
        plain_dot(normed, w_key).astype(jnp.bfloat16).reshape(batch_count, segment_len, key_width)
    )
    value_pre = (
        plain_dot(normed, w_value)
        .astype(jnp.bfloat16)
        .reshape(batch_count, segment_len, value_width)
    )
    gate_pre = plain_dot(normed, w_gate)
    rate_pre = plain_dot(normed, w_rate)
    behind = passed_along(
        (
            query_pre[:, segment_len - conv_lead :],
            key_pre[:, segment_len - conv_lead :],
            value_pre[:, segment_len - conv_lead :],
        ),
        "seq",
        1,
    )
    query_ext = jnp.concatenate([behind[0], query_pre], axis=1).astype(jnp.float32)
    key_ext = jnp.concatenate([behind[1], key_pre], axis=1).astype(jnp.float32)
    value_ext = jnp.concatenate([behind[2], value_pre], axis=1).astype(jnp.float32)
    prepared, prep_back = jax.vjp(
        prepare,
        query_ext,
        key_ext,
        value_ext,
        rate_pre.reshape(batch_count, segment_len, -1),
        conv_weight,
        decay_log,
        decay_bias,
    )
    queries, key_rows, values, beta_rows, decays = prepared
    queries = round_trip(queries)
    key_rows = round_trip(key_rows)
    values = round_trip(values)
    head_count = decay_log.shape[0]
    group_count = segment_len // GROUP

    def by_group(rows):
        moved = jnp.moveaxis(rows, 2, 1)
        return moved.reshape((batch_count, head_count, group_count, GROUP) + rows.shape[3:])

    def by_token(rows):
        joined = rows.reshape((batch_count, head_count, segment_len) + rows.shape[4:])
        return jnp.moveaxis(joined, 1, 2)

    (step_map, step_offset, read_map, read_offset), maps_back = jax.vjp(
        group_maps,
        by_group(queries),
        by_group(key_rows),
        by_group(values),
        by_group(beta_rows),
        by_group(decays),
    )
    maps = [step_map[:, :, g] for g in range(group_count)]
    offsets = [step_offset[:, :, g] for g in range(group_count)]
    mapping = maps[0]
    offset = offsets[0]
    for g in range(1, group_count):
        mapping = mid_dot(maps[g], mapping, "shij,shjk->shik")
        offset = mid_dot(maps[g], offset, "shij,shjk->shik") + offsets[g]
    entering = hop_sum(offset, 1)
    for hop_index in range(lax.axis_size("seq") - 2):
        entering = hop_sum(mid_dot(mapping, entering, "shij,shjk->shik") + offset, 1)
    states = [entering]
    for g in range(group_count - 1):
        states.append(mid_dot(maps[g], states[g], "shij,shjk->shik") + offsets[g])
    states = jnp.stack(states, axis=2)
    mixture = mid_dot(read_map, states, "shgtk,shgkv->shgtv") + read_offset
    gated_full, gate_back = jax.vjp(
        gate_output,
        by_token(mixture),
        gate_pre.reshape(batch_count, segment_len, value_width),
        out_gain,
    )
    gated = gated_full.reshape(row_count, value_width).astype(jnp.bfloat16)
    hidden = tokens + plain_dot(gated, w_output)
    normed_two_full, norm_two_back = jax.vjp(rms_scale, hidden, ffn_gain)
    normed_two = normed_two_full.astype(jnp.bfloat16)
    gate_vals = plain_dot(normed_two, w_ffgate)
    up_vals = plain_dot(normed_two, w_ffup)
    product_full, swiglu_back = jax.vjp(swiglu_product, gate_vals, up_vals)
    product = product_full.astype(jnp.bfloat16)
    outputs = (hidden + plain_dot(product, w_ffdown)).astype(jnp.bfloat16).reshape(inputs.shape)
    cotangent = upstream.reshape(row_count, model_width)
    product_grad = back_dot(cotangent, w_ffdown)
    grad_down = weight_dot(product, cotangent)
    gate_grad_full, up_grad_full = swiglu_back(product_grad)
    gate_grad = gate_grad_full.astype(jnp.bfloat16)
    up_grad = up_grad_full.astype(jnp.bfloat16)
    normed_two_grad = back_dot(gate_grad, w_ffgate) + back_dot(up_grad, w_ffup)
    grad_ffgate = weight_dot(normed_two, gate_grad)
    grad_ffup = weight_dot(normed_two, up_grad)
    hidden_part, ffn_gain_grad = norm_two_back(normed_two_grad)
    hidden_grad = cotangent.astype(jnp.float32) + hidden_part
    branch_grad = hidden_grad.astype(jnp.bfloat16)
    gated_grad = back_dot(branch_grad, w_output)
    grad_output = weight_dot(gated, branch_grad)
    mixture_grad_rows, gate_pre_grad, out_gain_grad = gate_back(
        gated_grad.reshape(batch_count, segment_len, value_width)
    )
    mixture_grad = by_group(mixture_grad_rows)
    read_grads = mid_dot(read_map, mixture_grad, "shgtk,shgtv->shgkv")
    reads = [read_grads[:, :, g] for g in range(group_count)]
    local_term = reads[group_count - 1]
    for g in range(group_count - 2, -1, -1):
        local_term = mid_dot(maps[g], local_term, "shji,shjk->shik") + reads[g]
    leaving = hop_sum(local_term, -1)
    for hop_index in range(lax.axis_size("seq") - 2):
        leaving = hop_sum(mid_dot(mapping, leaving, "shji,shjk->shik") + local_term, -1)
    after = [leaving]
    for g in range(group_count - 1, 0, -1):
        after.append(mid_dot(maps[g], after[-1], "shji,shjk->shik") + reads[g])
    after = jnp.stack(after[::-1], axis=2)
    query_grad, key_grad, value_grad, beta_grad, decay_grad = maps_back(
        (
            mid_dot(after, states, "shgkv,shgjv->shgkj"),
            after,
            mid_dot(mixture_grad, states, "shgtv,shgkv->shgtk"),
            mixture_grad,
        )
    )
    ext_grads = prep_back(
        (
            by_token(round_trip(query_grad)),
            by_token(round_trip(key_grad)),
            by_token(round_trip(value_grad)),
            by_token(beta_grad),
            by_token(decay_grad),
        )
    )
    (
        query_ext_grad,
        key_ext_grad,
        value_ext_grad,
        rate_grad_full,
        conv_grad,
        decay_log_grad,
        decay_bias_grad,
    ) = ext_grads
    returned = (
        passed_along(query_ext_grad[:, :conv_lead].astype(jnp.bfloat16), "seq", -1).astype(
            jnp.float32
        ),
        passed_along(key_ext_grad[:, :conv_lead].astype(jnp.bfloat16), "seq", -1).astype(
            jnp.float32
        ),
        passed_along(value_ext_grad[:, :conv_lead].astype(jnp.bfloat16), "seq", -1).astype(
            jnp.float32
        ),
    )

    def settle(ext_grad, incoming, channels):
        own_rows = ext_grad[:, conv_lead:]
        own_rows = jnp.concatenate(
            [
                own_rows[:, : segment_len - conv_lead],
                own_rows[:, segment_len - conv_lead :] + incoming,
            ],
            axis=1,
        )
        return own_rows.reshape(row_count, channels).astype(jnp.bfloat16)

    query_pre_grad = settle(query_ext_grad, returned[0], key_width)
    key_pre_grad = settle(key_ext_grad, returned[1], key_width)
    value_pre_grad = settle(value_ext_grad, returned[2], value_width)
    gate_pre_rounded = gate_pre_grad.reshape(row_count, value_width).astype(jnp.bfloat16)
    rate_grad = rate_grad_full.reshape(row_count, -1).astype(jnp.bfloat16)
    normed_grad = (
        back_dot(query_pre_grad, w_query)
        + back_dot(key_pre_grad, w_key)
        + back_dot(value_pre_grad, w_value)
        + back_dot(gate_pre_rounded, w_gate)
        + back_dot(rate_grad, w_rate)
    )
    grad_query = weight_dot(normed, query_pre_grad)
    grad_key = weight_dot(normed, key_pre_grad)
    grad_value = weight_dot(normed, value_pre_grad)
    grad_gate = weight_dot(normed, gate_pre_rounded)
    grad_rate = weight_dot(normed, rate_grad)
    token_part, norm_gain_grad = norm_back(normed_grad)
    input_grad = (hidden_grad + token_part).reshape(inputs.shape)
    summed = column_sums(
        tuple(
            row_sum(grad)
            for grad in (
                grad_query,
                grad_key,
                grad_value,
                grad_gate,
                grad_rate,
                grad_output,
                grad_ffgate,
                grad_ffup,
                grad_down,
            )
        )
    )
    small_grads = (
        norm_gain_grad,
        conv_grad,
        decay_log_grad,
        decay_bias_grad,
        out_gain_grad,
        ffn_gain_grad,
    )
    joined = lax.psum(jnp.concatenate([grad.reshape(-1) for grad in small_grads]), ("dp", "seq"))
    small_sums = []
    start = 0
    for grad in small_grads:
        small_sums.append(joined[start : start + grad.size].reshape(grad.shape))
        start = start + grad.size
    return (
        outputs,
        input_grad,
        small_sums[0],
        summed[0],
        summed[1],
        summed[2],
        summed[3],
        summed[4],
        small_sums[1],
        small_sums[2],
        small_sums[3],
        small_sums[4],
        summed[5],
        small_sums[5],
        summed[6],
        summed[7],
        summed[8],
    )


def solution(mesh):
    in_specs = (
        P(None, "dp", "seq", None),
        P(None, "dp", "seq", None),
        P(),
        P("dp", "seq"),
        P("dp", "seq"),
        P("dp", "seq"),
        P("dp", "seq"),
        P("dp", "seq"),
        P(),
        P(),
        P(),
        P(),
        P("dp", "seq"),
        P(),
        P("dp", "seq"),
        P("dp", "seq"),
        P("dp", "seq"),
    )
    out_specs = (
        P(None, "dp", "seq", None),
        P(None, "dp", "seq", None),
        P(),
        P("dp", "seq"),
        P("dp", "seq"),
        P("dp", "seq"),
        P("dp", "seq"),
        P("dp", "seq"),
        P(),
        P(),
        P(),
        P(),
        P("dp", "seq"),
        P(),
        P("dp", "seq"),
        P("dp", "seq"),
        P("dp", "seq"),
    )
    return jax.shard_map(shards, mesh=mesh, in_specs=in_specs, out_specs=out_specs, check_vma=False)
```

time: 2690 us -> 1360 us (0.51)
  matrix products: 1050 us -> 459 us
  waiting for transfers between devices: 867 us -> 544 us
  blocking collectives: 269 us -> 8.83 us
  other arithmetic: 223 us -> 134 us
  local copies, waits for them, and re-layouts: 188 us -> 147 us
  loops' own time: 40.7 us -> 0 us
    dot_general x274 -> x59, matrix products: 869 us -> 296 us  [the longest x51 271 us: mid_dot(): jnp.einsum(formula, left_mat, right_mat, precision=lax.Precision.HIGH)]
    reduce_scatter x15 -> x9, waiting for transfers between devices: 418 us -> 188 us  [the longest x8 159 us: row_sum(): lax.psum_scatter(grad.astype(jnp.bfloat16), 'dp', scatter_dimension=0, ti...]
    all_gather x10 -> x1, blocking collectives: 218 us -> 8.83 us  [gather_block(): lax.all_gather(rows[i].transpose(1, 0, 2).reshape(matrices[i].shape[0], -...]
    ppermute x12, waiting for transfers between devices: 285 us -> 118 us  [passed_along(): return lax.ppermute(block, axis, route)]
    all_gather x8 -> x10, waiting for transfers between devices: 0.07 us -> 89.6 us  [the longest x1 63.4 us: gather_block(): lax.all_gather(jnp.concatenate([matrices[i] for i in wide], axis=1), 'seq')]
    another operation x2 -> x0, loops' own time: 40.7 us -> none  [segment_terms(): lax.scan(group_step, initial, group_data)]
    psum x1 -> x0, blocking collectives: 39.5 us -> none  [shards(): lax.psum((norm_gain_grad, conv_grad, decay_log_grad, decay_bias_grad, out...]
    unnamed x28 -> x24, waiting for transfers between devices: 72.3 us -> 56.1 us
  transfers between devices with their start and end apart: 38 -> 34, of which waited for: 20 -> 18; matrix products, arithmetic and copies ran while one was open for 52% -> 48% of each run, Pallas kernels for 0% -> 0%
where the time goes in v1:
time: 1360 us
  waiting for transfers between devices  544 us (40%)
  matrix products  459 us (34%)
  local copies, waits for them, and re-layouts  147 us (11%)
  other arithmetic  134 us (10%)
  starting transfers between devices  45.3 us (3%)
  between operations  17.7 us (1%)
    dot_general x51, matrix products, mid_dot(): jnp.einsum(formula, left_mat, right_mat, precision=lax.Precision.HIGH)  271 us
    reduce_scatter x8, waiting for transfers between devices, row_sum(): lax.psum_scatter(grad.astype(jnp.bfloat16), 'dp', scatter_dimension=0, ti...  159 us
    ppermute x12, waiting for transfers between devices, passed_along(): return lax.ppermute(block, axis, route)  118 us
    psum x1, waiting for transfers between devices, shards(): lax.psum(jnp.concatenate([grad.reshape(-1) for grad in small_grads]), ('d...  93.1 us
    all_gather x1, waiting for transfers between devices, gather_block(): lax.all_gather(jnp.concatenate([matrices[i] for i in wide], axis=1), 'seq')  63.4 us
    dot_general x9, matrix products, plain_dot(): return jnp.dot(left_mat, right_mat, preferred_element_type=jnp.float32)  61.2 us
    unnamed x24, waiting for transfers between devices  56.1 us
    dot_general x9, matrix products, back_dot(): lax.dot_general(left_mat, right_mat, (((1,), (1,)), ((), ())), preferred_...  54 us
  transfers between devices with their start and end apart: 34, of which 18 were waited for; matrix products, arithmetic and copies ran while one was open for 48% of the time, Pallas kernels for 0%

profile of v1, /device:TPU:0, one launch (start us, length us, event | category | flops | bytes accessed | tf_op | source)
XLA Modules:
  0.0 1355.7 jit_solution(10918376496456746490)
XLA Ops:
  19.4 63.4 %all-gather.29.cloned.1.call-done = bf16[512,2948]{0,1:T(8,128)(2,1)} async-done(((bf16[128,2948]{0,1:T(8,128)(2,1)}), bf16[512,2948]{0,1:T(8,128)(2,1)}) %all-gather.29.cloned.1.call-update) | async-done | bytes 3018768 | tf_op jit(solution)/shard_map/all_gather | solution.py:162
  95.2 19.5 %all-gather.31.cloned.1.call-done = bf16[2432,256]{1,0:T(8,128)(2,1)} async-done(((bf16[608,256]{1,0:T(8,128)(2,1)}), bf16[2432,256]{1,0:T(8,128)(2,1)}) %all-gather.31.cloned.1.call-update) | async-done | bytes 1245200 | tf_op jit(solution)/shard_map/all_gather | solution.py:163
  126.5 8.8 all_gather.41
  153.6 11.1 all-gather.27.cloned.1.call-start
  238.9 9.8 fusion.29
  276.4 23.1 %collective-permute-done.3 = bf16[3,8,128,256]{3,2,1,0:T(8,128)(2,1)} collective-permute-done((bf16[3,8,128,256]{3,2,1,0:T(8,128)(2,1)}, bf16[3,8,128,256]{3,2,1,0:T(8,128)(2,1)}, u32[]{:S(2)}, u32[]{:S(2)}) %collective-permute-start.3) | collective-permute-done | bytes 1572896 | tf_op jit(solution)/shard_map/ppermute | solution.py:15
  310.9 13.9 %fusion.87 = (f32[3,256,1024]{2,1,0:T(8,128)S(1)}, f32[3,256,1024]{2,1,0:T(8,128)}) fusion(f32[3,259,1024]{2,1,0:T(8,128)S(1)} %maximum_convert_fusion.4, f32[1024]{0:T(1024)S(1)} %bitcast.682, f32[1024]{0:T(1024)S(1)} %bitcast.684, f32[1024]{0:T(1024)S(1)} %bitcast.686, f32[1024]{0:T(1024)S(1)} %bitcast.680), kind=kLoop, calls=%fused_computation.207 | loop fusion | flops 8650752 | bytes 18890752 | tf_op jit(solution)/shard_map/jvp(jit(silu))/mul | solution.py:70
  329.4 11.1 collective-permute-done.4
  365.0 16.6 %collective-permute-done.5 = bf16[3,8,128,256]{3,2,1,0:T(8,128)(2,1)} collective-permute-done((bf16[3,8,128,256]{3,2,1,0:T(8,128)(2,1)}, bf16[3,8,128,256]{3,2,1,0:T(8,128)(2,1)}, u32[]{:S(2)}, u32[]{:S(2)}) %collective-permute-start.5) | collective-permute-done | bytes 1572896 | tf_op jit(solution)/shard_map/ppermute | solution.py:15
  394.3 10.1 fusion.106
  407.1 9.5 multiply_convert_fusion.1
  429.8 10.1 fusion.261
  439.9 9.5 fusion.260
  449.4 17.3 %fusion.14 = (bf16[768,2816]{1,0:T(8,128)(2,1)}, bf16[768,2816]{1,0:T(8,128)(2,1)}, bf16[768,2816]{1,0:T(8,128)(2,1)}) fusion(f32[768,2816]{1,0:T(8,128)} %fusion.260, f32[768,2816]{1,0:T(8,128)} %fusion.261, bf16[2816,1024]{1,0:T(8,128)(2,1)} %all-gather.27.cloned.1.call-done, bf16[768,1024]{1,0:T(8,128)(2,1)} %bitcast.654), kind=kOutput, calls=%fused_computation.22 | convolution fusion | flops 4463788032 | bytes 37617664 | tf_op jit(solution)/shard_map/dot_general | solution.py:23
  499.0 9.5 multiply_reduce_fusion
  512.1 12.7 fusion.128
  542.8 31.4 %collective-permute-done.7 = bf16[3,8,128,256]{3,2,1,0:T(8,128)(2,1)S(1)} collective-permute-done((bf16[3,8,128,256]{3,2,1,0:T(8,128)(2,1)S(1)}, bf16[3,8,128,256]{3,2,1,0:T(8,128)(2,1)S(1)}, u32[]{:S(2)}, u32[]{:S(2)}) %collective-permute-start.7) | collective-permute-done | bytes 1572896 | tf_op jit(solution)/shard_map/ppermute | solution.py:15
  584.8 15.4 %fusion.34 = (f32[3,8,4,64]{3,2,1,0:T(4,128)}, f32[3,8,4,64,128]{4,3,2,1,0:T(8,128)}) fusion(bf16[3,8,4,64,128]{4,3,2,1,0:T(8,128)(2,1)S(1)} %bitcast.587, f32[3,8,4,64,256]{4,3,2,1,0:T(8,128)} %bitcast.565, f32[3,8,1,128,256]{4,3,1,0,2:T(8,128)} %add_bitcast_fusion.1, f32[3,8,1,128,256]{4,3,1,0,2:T(8,128)} %bitcast.595, ...), kind=kOutput, calls=%fused_computation.86 | convolution fusion | flops 1219749888 | bytes 23617536 | tf_op jit(solution)/shard_map/shgtv,shgkv->shgtk/dot_general | solution.py:35
  600.2 12.3 collective-permute-done.8
  638.0 14.6 %collective-permute-done.9 = bf16[3,8,128,256]{3,2,1,0:T(8,128)(2,1)} collective-permute-done((bf16[3,8,128,256]{3,2,1,0:T(8,128)(2,1)}, bf16[3,8,128,256]{3,2,1,0:T(8,128)(2,1)}, u32[]{:S(2)}, u32[]{:S(2)}) %collective-permute-start.9) | collective-permute-done | bytes 1572896 | tf_op jit(solution)/shard_map/ppermute | solution.py:15
  671.3 12.5 multiply_reduce_fusion.5
  705.5 12.8 fusion.41
  733.6 10.2 multiply_reduce_fusion.16
  864.2 9.0 convolution_convert_fusion.2
  959.3 44.2 %reduce-scatter.24.cloned.1.call-done = bf16[128,2816]{1,0:T(8,128)(2,1)} async-done(((bf16[1024,2816]{1,0:T(8,128)(2,1)}), bf16[128,2816]{1,0:T(8,128)(2,1)}) %reduce-scatter.24.cloned.1.call-update) | async-done | bytes 720912 | tf_op jit(solution)/shard_map/reduce_scatter | solution.py:184
  1004.9 61.3 %reduce-scatter.26.cloned.1.call-done = bf16[128,2816]{1,0:T(8,128)(2,1)} async-done(((bf16[1024,2816]{1,0:T(8,128)(2,1)}), bf16[128,2816]{1,0:T(8,128)(2,1)}) %reduce-scatter.26.cloned.1.call-update) | async-done | bytes 720912 | tf_op jit(solution)/shard_map/reduce_scatter | solution.py:184
  1067.7 53.3 %reduce-scatter.20.cloned.1.call-done = bf16[128,2048]{1,0:T(8,128)(2,1)} async-done(((bf16[1024,2048]{1,0:T(8,128)(2,1)}), bf16[128,2048]{1,0:T(8,128)(2,1)}) %reduce-scatter.20.cloned.1.call-update) | async-done | bytes 524304 | tf_op jit(solution)/shard_map/reduce_scatter | solution.py:184
  1123.0 17.4 %concatenate.42 = bf16[4,128,2948]{1,2,0:T(8,128)(2,1)} concatenate(bf16[4,128,256]{1,2,0:T(8,128)(2,1)} %bitcast.659, bf16[4,128,256]{1,2,0:T(8,128)(2,1)} %bitcast.658, bf16[4,128,512]{1,2,0:T(8,128)(2,1)} %bitcast.642, bf16[4,128,512]{1,2,0:T(8,128)(2,1)S(1)} %bitcast.640, bf16[4,128,4]{1,2,0:T(4,128)(2,1)S(1)} %bitcast.702, bf16[4,128,704]{1,2,0:T(8,128)(2,1)S(1)} %bitcast.634, ...), dimensions={2} | concatenate | bytes 6037504 | tf_op jit(solution)/shard_map/concatenate | solution.py:195
  1140.4 10.8 add_convert_fusion.4
  1153.7 93.1 %all-reduce.34.cloned.1.call-done = f32[18704]{0:T(1024)} async-done(((f32[18704]{0:T(1024)}), f32[18704]{0:T(1024)}) %all-reduce.34.cloned.1.call-update) | async-done | bytes 74832 | tf_op jit(solution)/shard_map/psum | solution.py:469
  1252.3 29.1 %reduce-scatter.32.cloned.1.call-done = bf16[1,608,256]{2,1,0:T(8,128)(2,1)} async-done(((bf16[4,608,256]{2,1,0:T(8,128)(2,1)}), bf16[1,608,256]{2,1,0:T(8,128)(2,1)}) %reduce-scatter.32.cloned.1.call-update) | async-done | bytes 311312 | tf_op jit(solution)/shard_map/reduce_scatter | solution.py:197
  1284.7 55.7 %reduce-scatter.36.cloned.1.call-done = bf16[1,128,2948]{1,2,0:T(8,128)(2,1)} async-done(((bf16[4,128,2948]{1,2,0:T(8,128)(2,1)}), bf16[1,128,2948]{1,2,0:T(8,128)(2,1)}) %reduce-scatter.36.cloned.1.call-update) | async-done | bytes 754704
  (746 shorter events, 599.2 us)
Async XLA Ops:
  7.2 75.6 %all-gather.29.cloned.1.call-start = ((), (), s32[]{:S(2)}) async-start(), calls=%async_computation.29 | async-start | bytes 3778560 | tf_op jit(solution)/shard_map/all_gather | solution.py:162
  18.5 96.2 %all-gather.31.cloned.1.call-start = ((), (), s32[]{:S(2)}) async-start(), calls=%async_computation.30 | async-start | bytes 1556480 | tf_op jit(solution)/shard_map/all_gather | solution.py:163
  19.4 125.1 %all-gather.15.cloned.1.call-start = ((), (), s32[]{:S(2)}) async-start(), calls=%async_computation.12 | async-start | bytes 2359296 | tf_op jit(solution)/shard_map/all_gather | solution.py:176
  88.9 121.1 %all-gather.17.cloned.1.call-start = ((), (), s32[]{:S(2)}) async-start(), calls=%async_computation.13 | async-start | bytes 4718592 | tf_op jit(solution)/shard_map/all_gather | solution.py:176
  92.1 176.1 %all-gather.13.cloned.1.call-start = ((), (), s32[]{:S(2)}) async-start(), calls=%async_computation.11 | async-start | bytes 2359296 | tf_op jit(solution)/shard_map/all_gather | solution.py:176
  93.0 314.1 %all-gather.19.cloned.1.call-start = ((), (), s32[]{:S(2)}) async-start(), calls=%async_computation.14 | async-start | bytes 4718592 | tf_op jit(solution)/shard_map/all_gather | solution.py:176
  95.1 326.1 %all-gather.21.cloned.1.call-start = ((), (), s32[]{:S(2)}) async-start(), calls=%async_computation.15 | async-start | bytes 4718592 | tf_op jit(solution)/shard_map/all_gather | solution.py:176
  116.9 312.9 %all-gather.25.cloned.1.call-start = ((), (), s32[]{:S(2)}) async-start(), calls=%async_computation.17 | async-start | bytes 6488064 | tf_op jit(solution)/shard_map/all_gather | solution.py:176
  120.4 319.5 %all-gather.23.cloned.1.call-start = ((), (), s32[]{:S(2)}) async-start(), calls=%async_computation.16 | async-start | bytes 6488064 | tf_op jit(solution)/shard_map/all_gather | solution.py:176
  148.4 16.3 %collective-permute-start.1 = (bf16[3,3,1024]{2,1,0:T(4,128)(2,1)S(1)}, bf16[3,3,1024]{2,1,0:T(4,128)(2,1)S(1)}, u32[]{:S(2)}, u32[]{:S(2)}) collective-permute-start(bf16[3,3,1024]{2,1,0:T(4,128)(2,1)S(1)} %slice.342), channel_id=1, source_target_pairs={{0,1},{1,2},{2,3},{4,5},{5,6},{6,7},{8,9},{9,10},{10,11},{12,13},{... | collective-permute-start | bytes 55304 | tf_op jit(solution)/shard_map/ppermute | solution.py:15
  153.6 295.9 %all-gather.27.cloned.1.call-start = ((), (), s32[]{:S(2)}) async-start(), calls=%async_computation.18 | async-start | bytes 6488064 | tf_op jit(solution)/shard_map/all_gather | solution.py:176
  216.3 10.8 collective-permute-start.2
  262.0 37.5 %collective-permute-start.3 = (bf16[3,8,128,256]{3,2,1,0:T(8,128)(2,1)}, bf16[3,8,128,256]{3,2,1,0:T(8,128)(2,1)}, u32[]{:S(2)}, u32[]{:S(2)}) collective-permute-start(bf16[3,8,128,256]{3,2,1,0:T(8,128)(2,1)} %get-tuple-element.249), channel_id=1, source_target_pairs={{0,1},{1,2},{2,3},{4,5},{5,6},{6,7},{8,9},{9,10},{10,11},{12,13},{... | collective-permute-start | bytes 4718600 | tf_op jit(solution)/shard_map/ppermute | solution.py:15
  272.2 38.0 %collective-permute-start = (bf16[3,3,1024]{2,1,0:T(4,128)(2,1)S(1)}, bf16[3,3,1024]{2,1,0:T(4,128)(2,1)S(1)}, u32[]{:S(2)}, u32[]{:S(2)}) collective-permute-start(bf16[3,3,1024]{2,1,0:T(4,128)(2,1)S(1)} %slice.336), channel_id=1, source_target_pairs={{0,1},{1,2},{2,3},{4,5},{5,6},{6,7},{8,9},{9,10},{10,11},{12,13},{... | collective-permute-start | bytes 55304 | tf_op jit(solution)/shard_map/ppermute | solution.py:15
  303.3 37.2 %collective-permute-start.4 = (bf16[3,8,128,256]{3,2,1,0:T(8,128)(2,1)}, bf16[3,8,128,256]{3,2,1,0:T(8,128)(2,1)}, u32[]{:S(2)}, u32[]{:S(2)}) collective-permute-start(bf16[3,8,128,256]{3,2,1,0:T(8,128)(2,1)} %add_convert_fusion.6), channel_id=1, source_target_pairs={{0,1},{1,2},{2,3},{4,5},{5,6},{6,7},{8,9},{9,10},{10,11},{12,13},{... | collective-permute-start | bytes 4718600 | tf_op jit(solution)/shard_map/ppermute | solution.py:15
  310.2 639.3 %reduce-scatter.28.cloned.1.call-start = ((), (), s32[]{:S(2)}) async-start(), calls=%async_computation.26 | async-start | bytes 4718592 | tf_op jit(solution)/shard_map/reduce_scatter | solution.py:184
  345.7 36.0 %collective-permute-start.5 = (bf16[3,8,128,256]{3,2,1,0:T(8,128)(2,1)}, bf16[3,8,128,256]{3,2,1,0:T(8,128)(2,1)}, u32[]{:S(2)}, u32[]{:S(2)}) collective-permute-start(bf16[3,8,128,256]{3,2,1,0:T(8,128)(2,1)} %add_convert_fusion.5), channel_id=1, source_target_pairs={{0,1},{1,2},{2,3},{4,5},{5,6},{6,7},{8,9},{9,10},{10,11},{12,13},{... | collective-permute-start | bytes 4718600 | tf_op jit(solution)/shard_map/ppermute | solution.py:15
  489.1 461.6 %reduce-scatter.30.cloned.1.call-start = ((), (), s32[]{:S(2)}) async-start(), calls=%async_computation.27 | async-start | bytes 6488064 | tf_op jit(solution)/shard_map/reduce_scatter | solution.py:184
  537.0 37.2 %collective-permute-start.7 = (bf16[3,8,128,256]{3,2,1,0:T(8,128)(2,1)S(1)}, bf16[3,8,128,256]{3,2,1,0:T(8,128)(2,1)S(1)}, u32[]{:S(2)}, u32[]{:S(2)}) collective-permute-start(bf16[3,8,128,256]{3,2,1,0:T(8,128)(2,1)S(1)} %get-tuple-element.256), channel_id=1, source_target_pairs={{1,0},{2,1},{3,2},{5,4},{6,5},{7,6},{9,8},{10,9},{11,10},{13,12},{... | collective-permute-start | bytes 4718600 | tf_op jit(solution)/shard_map/ppermute | solution.py:15
  576.7 35.8 %collective-permute-start.8 = (bf16[3,8,128,256]{3,2,1,0:T(8,128)(2,1)}, bf16[3,8,128,256]{3,2,1,0:T(8,128)(2,1)}, u32[]{:S(2)}, u32[]{:S(2)}) collective-permute-start(bf16[3,8,128,256]{3,2,1,0:T(8,128)(2,1)} %add_convert_fusion.2), channel_id=1, source_target_pairs={{1,0},{2,1},{3,2},{5,4},{6,5},{7,6},{9,8},{10,9},{11,10},{13,12},{... | collective-permute-start | bytes 4718600 | tf_op jit(solution)/shard_map/ppermute | solution.py:15
  584.6 368.8 %reduce-scatter.34.cloned.1.call-start = ((), (), s32[]{:S(2)}) async-start(), calls=%async_computation.31 | async-start | bytes 294912
  617.4 35.3 %collective-permute-start.9 = (bf16[3,8,128,256]{3,2,1,0:T(8,128)(2,1)}, bf16[3,8,128,256]{3,2,1,0:T(8,128)(2,1)}, u32[]{:S(2)}, u32[]{:S(2)}) collective-permute-start(bf16[3,8,128,256]{3,2,1,0:T(8,128)(2,1)} %add_convert_fusion.1), channel_id=1, source_target_pairs={{1,0},{2,1},{3,2},{5,4},{6,5},{7,6},{9,8},{10,9},{11,10},{13,12},{... | collective-permute-start | bytes 4718600 | tf_op jit(solution)/shard_map/ppermute | solution.py:15
  763.4 190.9 %reduce-scatter.22.cloned.1.call-start = ((), (), s32[]{:S(2)}) async-start(), calls=%async_computation.23 | async-start | bytes 4718592 | tf_op jit(solution)/shard_map/reduce_scatter | solution.py:184
  770.4 185.2 %reduce-scatter.18.cloned.1.call-start = ((), (), s32[]{:S(2)}) async-start(), calls=%async_computation.21 | async-start | bytes 2359296 | tf_op jit(solution)/shard_map/reduce_scatter | solution.py:184
  834.7 122.8 %reduce-scatter.16.cloned.1.call-start = ((), (), s32[]{:S(2)}) async-start(), calls=%async_computation.20 | async-start | bytes 2359296 | tf_op jit(solution)/shard_map/reduce_scatter | solution.py:184
  864.1 139.4 %reduce-scatter.24.cloned.1.call-start = ((), (), s32[]{:S(2)}) async-start(), calls=%async_computation.24 | async-start | bytes 6488064 | tf_op jit(solution)/shard_map/reduce_scatter | solution.py:184
  873.2 193.1 %reduce-scatter.26.cloned.1.call-start = ((), (), s32[]{:S(2)}) async-start(), calls=%async_computation.25 | async-start | bytes 6488064 | tf_op jit(solution)/shard_map/reduce_scatter | solution.py:184
  882.0 238.9 %reduce-scatter.20.cloned.1.call-start = ((), (), s32[]{:S(2)}) async-start(), calls=%async_computation.22 | async-start | bytes 4718592 | tf_op jit(solution)/shard_map/reduce_scatter | solution.py:184
  915.0 6.0 collective-permute-start.11
  928.2 318.6 %all-reduce.34.cloned.1.call-start = ((), (), s32[]{:S(2)}) async-start(), calls=%async_computation.19 | async-start | bytes 155648 | tf_op jit(solution)/shard_map/psum | solution.py:469
  949.5 331.9 %reduce-scatter.32.cloned.1.call-start = ((), (), s32[]{:S(2)}) async-start(), calls=%async_computation.28 | async-start | bytes 1556480 | tf_op jit(solution)/shard_map/reduce_scatter | solution.py:197
  953.1 387.3 %reduce-scatter.36.cloned.1.call-start = ((), (), s32[]{:S(2)}) async-start(), calls=%async_computation.32 | async-start | bytes 3778560
  (206 other events, 2707.9 us)
Sparse Core Ops, SparseCore 0:
  18.6 64.0 all-gather.28
  84.9 29.7 all-gather.30
  117.2 27.2 all-gather.14
  146.2 37.4 all-gather.16
  186.0 28.1 all-gather.12
  216.0 37.4 all-gather.18
  255.3 37.4 all-gather.20
  294.7 44.3 all-gather.24
  340.9 44.3 all-gather.22
  387.1 43.3 all-gather.26
  489.3 51.8 reduce-scatter.27
  584.7 61.6 reduce-scatter.29
  763.5 33.4 reduce-scatter.33
  800.6 51.2 reduce-scatter.21
  855.0 41.2 reduce-scatter.17
  899.8 41.2 reduce-scatter.15
  944.4 59.0 reduce-scatter.23
  1007.2 59.0 reduce-scatter.25
  1069.6 51.3 reduce-scatter.19
  1127.9 118.8 all-reduce.33
  1249.2 32.1 reduce-scatter.31
  1283.7 56.6 reduce-scatter.35
